TPU v7x, 32 devices: a whole 2x2x4 slice. The times are simulated.
32 devices in a mesh: dp: 4 (over y, x), exp: 8 (over z, core).
Axes of the slice: x: 2, y: 2, z: 4, core: 2. Of those that a mesh axis runs over, the one named last changes fastest.
Arguments:
- hidden: bfloat16 [4096, 2048], P(('dp', 'exp')), may hold values from -6 to 6
- queries: bfloat16 [4096, 2048], P(('dp', 'exp')), may hold values from -1000 to 1000
- draft_entries: bfloat16 [2, 4096, 512], P(None, ('dp', 'exp')), may hold values from -6 to 6
- key_pool: bfloat16 [256, 64, 512], P(('dp', 'exp')), may hold values from -8 to 8
- value_pool: bfloat16 [256, 64, 512], P(('dp', 'exp')), may hold values from -6 to 6
- page_table: int32 [64, 4], P(('dp', 'exp')), may hold values from 0 to 31, as said below
- cache_len: int32 [64], P(('dp', 'exp')), may hold values from 2 to 256, as said below
- parents: int32 [64, 64], P(('dp', 'exp')), may hold values from -1 to 62, as said below
- out_proj: bfloat16 [2048, 2048], replicated, may hold values from -0.125 to 0.125
- norm_gain: bfloat16 [2048], replicated, may hold values from 0.099609375 to 1.8984375
- expert_gate: bfloat16 [64, 1408, 2048], P('exp', 'dp'), may hold values from -0.125 to 0.125
- expert_up: bfloat16 [64, 1408, 2048], P('exp', 'dp'), may hold values from -0.125 to 0.125
- expert_down: bfloat16 [64, 1408, 2048], P('exp', 'dp'), may hold values from -0.15625 to 0.15625
- shared_gate: bfloat16 [1408, 2048], P('dp'), may hold values from -0.125 to 0.125
- shared_up: bfloat16 [1408, 2048], P('dp'), may hold values from -0.125 to 0.125
- shared_down: bfloat16 [1408, 2048], P('dp'), may hold values from -0.15625 to 0.15625
- expert_ids: int32 [4096, 6], P(('dp', 'exp')), may hold values from 0 to 63, all different within a row; in each aligned block of 128 rows (0 to 127, 128 to 255, ...) at most 16 rows name the same one
- expert_weights: float32 [4096, 6], P(('dp', 'exp')), may hold values from 0.05 to 0.5
Outputs:
- verified: bfloat16 [4096, 2048], P(('dp', 'exp'))
Inputs may be any that keep to these rules, and one draw needn't show every extreme that they name: `page_table`: page ids count within the 4 devices that share the request's index of exp: page q lies on the one of dp index q // 8, as its page q % 8; the requests of those devices together use each of their 32 pages exactly once. `cache_len`: some request has exactly 256 cached positions. parents[r, i] is -1 or an earlier node i' < i of the same request; parents[r, 0] = -1. `expert_ids`: each row names 6 different experts; the 128 rows of one device name one expert at most 16 times, a bound that some block reaches.
All inputs are finite; a program needn't handle non-finite values.
Results may differ from a plain program's by a relative error of at most 0.015.
Values may be sent and summed in bfloat16 or wider, within the bound.
A program may use at most 192 MiB of HBM per device.

v0:
```python
import jax
import jax.numpy as jnp
from jax import lax
from jax.sharding import PartitionSpec as P

HEADS = 16
KVH = 4
HD = 128
CAP = 16


NEG_FILL = -1e30
NORM_EPSILON = 1e-06
HIGHEST_PRECISION = lax.Precision.HIGHEST


def tree_reach(parents):
    node_count = parents.shape[-1]
    node_index = jnp.arange(node_count, dtype=jnp.int32)
    linked = (parents[:, :, None] == node_index[None, None, :]).astype(jnp.float32)
    reached = jnp.minimum(linked + jnp.eye(node_count, dtype=jnp.float32)[None], 1.0)
    for rounds in range(max(1, (node_count - 1).bit_length())):
        reached = jnp.minimum(
            jnp.einsum("rij,rjk->rik", reached, reached, precision=HIGHEST_PRECISION), 1.0
        )
    return reached


def score_block(query_heads, key_rows, live_mask):
    raw_scores = jnp.einsum(
        "rtgnd,rcgd->rgntc", query_heads, key_rows, preferred_element_type=jnp.float32
    ) * key_rows.shape[-1] ** (-0.5)
    wide_mask = live_mask[:, None, None]
    return (jnp.where(wide_mask, raw_scores, NEG_FILL), wide_mask)


def fold_keys(carry_state, scores, wide_mask, value_rows):
    running_top, running_total, running_sum = carry_state
    fresh_top = jnp.maximum(running_top, jnp.max(scores, axis=-1))
    rescale = jnp.exp(running_top - fresh_top)
    exponents = jnp.where(wide_mask, jnp.exp(scores - fresh_top[..., None]), 0.0)
    weights = exponents.astype(jnp.bfloat16)
    new_total = running_total * rescale + jnp.sum(exponents, axis=-1)
    mixed = jnp.einsum("rgntc,rcgd->rtgnd", weights, value_rows, preferred_element_type=jnp.float32)
    new_sum = running_sum * jnp.transpose(rescale, (0, 3, 1, 2))[..., None] + mixed
    return (fresh_top, new_total, new_sum)


def pool_state(carry_state, query_heads, table_rows, lengths, pieces):
    piece_keys, piece_values = pieces
    piece_count = piece_keys.shape[0]
    request_count, pages_per = table_rows.shape
    page_size = piece_keys.shape[1]
    key_heads = query_heads.shape[2]
    inside = (table_rows >= 0) & (table_rows < piece_count)
    picked = jnp.clip(table_rows, 0, piece_count - 1)
    cache_keys = piece_keys[picked].reshape(request_count, pages_per * page_size, key_heads, -1)
    cache_values = piece_values[picked].reshape(request_count, pages_per * page_size, key_heads, -1)
    positions = jnp.arange(pages_per * page_size, dtype=jnp.int32)
    usable = jnp.repeat(inside, page_size, axis=1) & (positions[None, :] < lengths[:, None])
    live_mask = jnp.broadcast_to(
        usable[:, None, :], (request_count, query_heads.shape[1], pages_per * page_size)
    )
    scores, wide_mask = score_block(query_heads, cache_keys, live_mask)
    return fold_keys(carry_state, scores, wide_mask, cache_values)


def blank_state(request_count, draft_nodes, key_heads, group_size, head_size):
    return (
        jnp.full((request_count, key_heads, group_size, draft_nodes), NEG_FILL, jnp.float32),
        jnp.zeros((request_count, key_heads, group_size, draft_nodes), jnp.float32),
        jnp.zeros((request_count, draft_nodes, key_heads, group_size, head_size), jnp.float32),
    )


def expert_block(grouped, gate_rows, upper_rows, down_rows):
    gate_values = jnp.einsum(
        "sekd,efd->sekf", grouped, gate_rows, preferred_element_type=jnp.float32
    )
    upper_values = jnp.einsum(
        "sekd,efd->sekf", grouped, upper_rows, preferred_element_type=jnp.float32
    )
    inner = (jax.nn.silu(gate_values) * upper_values).astype(jnp.bfloat16)
    return jnp.einsum("sekf,efd->sekd", inner, down_rows, preferred_element_type=jnp.float32)


def shared_block(tokens, gate_rows, upper_rows, down_rows):
    gate_values = jnp.einsum("td,fd->tf", tokens, gate_rows, preferred_element_type=jnp.float32)
    upper_values = jnp.einsum("td,fd->tf", tokens, upper_rows, preferred_element_type=jnp.float32)
    inner = (jax.nn.silu(gate_values) * upper_values).astype(jnp.bfloat16)
    return jnp.dot(inner, down_rows, preferred_element_type=jnp.float32)


def on_device(
    hidden,
    queries,
    draft_entries,
    key_pool,
    value_pool,
    page_table,
    cache_len,
    parents,
    out_proj,
    norm_gain,
    expert_gate,
    expert_up,
    expert_down,
    shared_gate,
    shared_up,
    shared_down,
    expert_ids,
    expert_weights,
):
    tok_rows, model_width = hidden.shape
    local_requests, draft_nodes = parents.shape
    group_size = HEADS // KVH
    query_heads = queries.reshape(local_requests, draft_nodes, KVH, group_size, HD)
    draft_keys = draft_entries[0].reshape(local_requests, draft_nodes, KVH, HD)
    draft_values = draft_entries[1].reshape(local_requests, draft_nodes, KVH, HD)
    reached = tree_reach(parents)
    tree_scores, tree_mask = score_block(query_heads, draft_keys, reached > 0.5)
    tree_state = fold_keys(
        blank_state(local_requests, draft_nodes, KVH, group_size, HD),
        tree_scores,
        tree_mask,
        draft_values,
    )
    final_top, final_total, final_sum = pool_state(
        tree_state,
        query_heads,
        page_table,
        cache_len,
        (
            lax.all_gather(key_pool, "dp", axis=0, tiled=True),
            lax.all_gather(value_pool, "dp", axis=0, tiled=True),
        ),
    )
    attention = (
        (final_sum / jnp.transpose(final_total, (0, 3, 1, 2))[..., None])
        .reshape(tok_rows, queries.shape[1])
        .astype(jnp.bfloat16)
    )
    residual = (
        hidden.astype(jnp.float32)
        + jnp.dot(attention, out_proj, preferred_element_type=jnp.float32)
    ).astype(jnp.bfloat16)
    residual_wide = residual.astype(jnp.float32)
    scale_rows = lax.rsqrt(
        jnp.mean(residual_wide * residual_wide, axis=-1, keepdims=True) + NORM_EPSILON
    )
    normed = (residual_wide * scale_rows * norm_gain.astype(jnp.float32)).astype(jnp.bfloat16)
    local_experts = expert_gate.shape[0]
    column_count = lax.axis_size("exp")
    expert_count = local_experts * column_count
    pick_count = expert_ids.shape[1]
    flat_experts = expert_ids.reshape(-1)
    onehot = (flat_experts[:, None] == jnp.arange(expert_count, dtype=jnp.int32)[None, :]).astype(
        jnp.int32
    )
    slot_ids = jnp.sum((jnp.cumsum(onehot, axis=0) - 1) * onehot, axis=1)
    destinations = flat_experts * CAP + slot_ids
    token_rows = jnp.arange(tok_rows * pick_count, dtype=jnp.int32) // pick_count
    outgoing = (
        jnp.zeros((expert_count * CAP, model_width), jnp.bfloat16)
        .at[destinations]
        .set(normed[token_rows])
    )
    outgoing = outgoing.reshape(column_count, local_experts, CAP, model_width)
    arrived = lax.all_to_all(outgoing, "exp", split_axis=0, concat_axis=0, tiled=True)
    grouped, group_tokens = (
        lax.all_gather(arrived, "dp", axis=0, tiled=True),
        lax.all_gather(normed, "dp", axis=0, tiled=True),
    )
    routed_terms = expert_block(grouped, expert_gate, expert_up, expert_down)
    shared_terms = shared_block(group_tokens, shared_gate, shared_up, shared_down)
    routed_sum, shared_sum = (
        lax.psum_scatter(
            routed_terms.astype(jnp.bfloat16), "dp", scatter_dimension=0, tiled=True
        ).astype(jnp.float32),
        lax.psum_scatter(
            shared_terms.astype(jnp.bfloat16), "dp", scatter_dimension=0, tiled=True
        ).astype(jnp.float32),
    )
    returned = lax.all_to_all(
        routed_sum.astype(jnp.bfloat16), "exp", split_axis=0, concat_axis=0, tiled=True
    )
    returned_rows = returned.reshape(expert_count * CAP, model_width)
    picked_rows = (
        returned_rows[destinations].astype(jnp.float32).reshape(tok_rows, pick_count, model_width)
    )
    routed_out = jnp.sum(picked_rows * expert_weights[:, :, None], axis=1)
    return (residual.astype(jnp.float32) + routed_out + shared_sum).astype(jnp.bfloat16)


def solution(mesh):
    placed = (
        P(("dp", "exp"), None),
        P(("dp", "exp"), None),
        P(None, ("dp", "exp"), None),
        P(("dp", "exp"), None, None),
        P(("dp", "exp"), None, None),
        P(("dp", "exp"), None),
        P(("dp", "exp")),
        P(("dp", "exp"), None),
        P(),
        P(),
        P("exp", "dp", None),
        P("exp", "dp", None),
        P("exp", "dp", None),
        P("dp", None),
        P("dp", None),
        P("dp", None),
        P(("dp", "exp"), None),
        P(("dp", "exp"), None),
    )
    return jax.shard_map(
        on_device, mesh=mesh, in_specs=placed, out_specs=P(("dp", "exp"), None), check_vma=False
    )
```

profile of v0, /device:TPU:0, one launch (start us, length us, event | category | flops | bytes accessed | tf_op | source)
XLA Modules:
  0.0 865.3 jit_solution(8510292942380966115)
XLA Ops:
  6.6 0.7 all-gather.5.cloned.1.call-update
  7.3 0.7 all-gather.7.cloned.1.call-update
  8.1 0.7 compare_and_fusion.1
  8.8 0.7 compare_select_fusion.2
  9.5 0.8 copy.52
  10.3 0.1 eq.53
  10.4 0.1 eq.49
  10.8 1.4 reshape.147
  12.2 1.0 convolution_minimum_fusion.5
  13.2 0.2 convolution_minimum_fusion.4
  13.4 0.2 convolution_minimum_fusion.3
  13.6 0.2 convolution_minimum_fusion.2
  13.8 0.2 convolution_minimum_fusion.1
  14.0 0.2 fusion.30
  14.2 0.1 copy.42
  14.4 0.7 reshape_squeeze.7
  15.1 0.6 convert_element_type.83
  15.7 1.8 reduce-window.6
  17.5 0.3 slice_reduce_fusion
  17.8 0.1 copy.51
  17.9 0.1 mul.104
  18.1 0.6 pad_clamp_fusion.2
  18.7 0.6 pad_clamp_fusion.1
  19.3 0.1 fusion.56
  19.4 0.6 fusion.71
  20.1 0.7 compare_and_fusion
  20.7 1.3 fusion.83
  22.0 25.3 %all-gather.5.cloned.1.call-done = bf16[32,64,512]{2,1,0:T(8,128)(2,1)} async-done(((bf16[8,64,512]{2,1,0:T(8,128)(2,1)}), bf16[32,64,512]{2,1,0:T(8,128)(2,1)}) %all-gather.5.cloned.1.call-update) | async-done | bytes 2097168 | tf_op jit(solution)/shard_map/all_gather | solution.py:134
  47.3 2.3 gather_fusion
  49.6 0.9 reshape.149
  50.5 34.0 %all-gather.7.cloned.1.call-done = bf16[32,64,512]{2,1,0:T(8,128)(2,1)} async-done(((bf16[8,64,512]{2,1,0:T(8,128)(2,1)}), bf16[32,64,512]{2,1,0:T(8,128)(2,1)}) %all-gather.7.cloned.1.call-update) | async-done | bytes 2097168 | tf_op jit(solution)/shard_map/all_gather | solution.py:135
  84.5 2.3 gather_fusion.1
  86.8 0.9 reshape.150
  87.7 1.7 bitcast_reduce_fusion
  89.4 0.9 fusion.20
  90.3 0.8 convolution_bitcast_fusion.1
  91.1 0.3 fusion.38
  91.5 1.2 fusion.28
  92.7 0.4 copy.50
  93.1 0.4 convert_element_type.79
  93.5 4.8 multiply_reduce_fusion.1
  98.3 0.2 multiply_convert_fusion
  98.5 23.1 %scatter_custom_fusion = bf16[1024,2048]{1,0:T(8,128)(2,1)} fusion(s32[768]{0:T(1024)S(1)} %copy-done.9, bf16[128,2048]{1,0:T(8,128)(2,1)S(1)} %multiply_convert_fusion, s32[1024]{0:T(1024)} %pad_clamp_fusion.1, bf16[]{:T(256)} %constant.12.clone.1), kind=kCustom, calls=%fused_computation.19 | custom fusion | bytes 4194816 | tf_op jit(solution)/shard_map/scatter | solution.py:166
  121.6 98.9 %all_to_all.10 = bf16[8,8,16,2048]{3,2,1,0:T(8,128)(2,1)S(1)} all-to-all(bf16[8,8,16,2048]{3,2,1,0:T(8,128)(2,1)} %bitcast.141), channel_id=1, replica_groups=mesh['dp'=4,'exp'=8] {'exp'}, dimensions={0} | all-to-all | bytes 8388608 | tf_op jit(solution)/shard_map/all_to_all | solution.py:169
  220.5 2.2 copy.55
  222.8 155.4 %all-gather.9.cloned.1.call-done = bf16[32,8,16,2048]{3,2,0,1:T(8,128)(2,1)} async-done(((bf16[8,8,16,2048]{3,2,0,1:T(8,128)(2,1)}), bf16[32,8,16,2048]{3,2,0,1:T(8,128)(2,1)}) %all-gather.9.cloned.1.call-update) | async-done | bytes 16777232 | tf_op jit(solution)/shard_map/all_gather | solution.py:171
  378.2 17.3 %fusion.1 = f32[8,32,16,352]{3,2,1,0:T(8,128)} fusion(bf16[32,8,16,2048]{3,2,0,1:T(8,128)(2,1)} %all-gather.9.cloned.1.call-done, bf16[8,352,2048]{2,1,0:T(8,128)(2,1)} %param.29), kind=kOutput, calls=%fused_computation.7 | convolution fusion | flops 5905580032 | bytes 34078720 | tf_op jit(solution)/shard_map/sekd,efd->sekf/dot_general | solution.py:80
  395.5 26.4 %convert_bitcast_fusion = bf16[32,8,16,2048]{3,2,0,1:T(8,128)(2,1)} fusion(bf16[8,352,2048]{2,1,0:T(8,128)(2,1)} %param.30, f32[8,32,16,352]{3,2,1,0:T(8,128)} %fusion.1, bf16[32,8,16,2048]{3,2,0,1:T(8,128)(2,1)} %all-gather.9.cloned.1.call-done, bf16[8,352,2048]{2,1,0:T(8,128)(2,1)} %param.28), kind=kOutput, calls=%fused_computation.5 | convolution fusion | flops 11828199424 | bytes 62390272 | tf_op jit(solution)/shard_map/sekf,efd->sekd/dot_general | solution.py:84
  422.0 0.5 all-gather.11.cloned.1.call-update
  422.6 0.6 dynamic-slice
  423.8 305.8 %all-reduce.3.cloned.1.call-done = bf16[32,8,16,2048]{3,2,0,1:T(8,128)(2,1)} async-done(((bf16[32,8,16,2048]{3,2,0,1:T(8,128)(2,1)}), bf16[32,8,16,2048]{3,2,0,1:T(8,128)(2,1)}) %all-reduce.3.cloned.1.call-update) | async-done | bytes 16777232
  729.5 2.5 constant_dynamic-slice_fusion
  732.0 2.3 copy.56
  734.3 4.6 all-to-all-start.1
  738.9 0.3 reduce-scatter.5.cloned.1.call-start
  739.2 28.5 %all-gather.11.cloned.1.call-done = bf16[512,2048]{1,0:T(8,128)(2,1)} async-done(((bf16[128,2048]{1,0:T(8,128)(2,1)}), bf16[512,2048]{1,0:T(8,128)(2,1)}) %all-gather.11.cloned.1.call-update) | async-done | bytes 2097168 | tf_op jit(solution)/shard_map/all_gather | solution.py:172
  767.8 2.9 fusion.84
  770.7 5.7 convolution_convert_fusion
  776.4 0.7 copy.57
  777.2 55.9 %all-to-all-done.1 = bf16[8,8,16,2048]{3,2,1,0:T(8,128)(2,1)} async-done(((bf16[8,8,16,2048]{3,2,1,0:T(8,128)(2,1)}), bf16[8,8,16,2048]{3,2,1,0:T(8,128)(2,1)}, u32[]{:S(2)}, u32[]{:S(2)}) %all-to-all-start.1) | async-done | bytes 4194336 | tf_op jit(solution)/shard_map/all_to_all | solution.py:184
  833.0 9.8 %gather_fusion.2 = bf16[768,2048]{1,0:T(8,128)(2,1)} fusion(bf16[1024,2048]{1,0:T(8,128)(2,1)} %bitcast.23, s32[1024]{0:T(1024)S(1)} %pad_clamp_fusion), kind=kCustom, calls=%fused_computation.3 | custom fusion | bytes 6294528 | tf_op jit(solution)/shard_map/gather | solution.py:189
  842.9 6.6 reshape.154
  849.4 6.5 multiply_reduce_fusion
  856.0 2.0 add_convert_fusion
  (53 shorter events, 0.8 us)
Async XLA Ops:
  6.5 764.2 %copy-start = (bf16[352,2048]{1,0:T(8,128)(2,1)S(1)}, bf16[352,2048]{1,0:T(8,128)(2,1)}, u32[]{:S(2)}) copy-start(bf16[352,2048]{1,0:T(8,128)(2,1)} %param.33) | copy-start | bytes 4325380
  6.5 11.3 %copy-start.8 = (s32[128,6]{0,1:T(8,128)S(1)}, s32[128,6]{0,1:T(8,128)}, u32[]{:S(2)}) copy-start(s32[128,6]{0,1:T(8,128)} %param.34) | copy-start | bytes 9220
  6.5 7.8 copy-start.4
  6.5 8.6 copy-start.11
  6.5 13.5 %copy-start.13 = (s32[2]{0:T(128)S(1)}, s32[2]{0:T(128)}, u32[]{:S(2)}) copy-start(s32[2]{0:T(128)} %param.24) | copy-start | bytes 28
  6.5 40.7 %all-gather.5.cloned.1.call-start = ((), (), s32[]{:S(2)}) async-start(), calls=%async_computation.3 | async-start | bytes 2621440 | tf_op jit(solution)/shard_map/all_gather | solution.py:134
  7.3 77.2 %all-gather.7.cloned.1.call-start = ((), (), s32[]{:S(2)}) async-start(), calls=%async_computation.4 | async-start | bytes 2621440 | tf_op jit(solution)/shard_map/all_gather | solution.py:135
  8.0 370.2 %all-gather.9.cloned.1.call-start = ((), (), s32[]{:S(2)}) async-start(), calls=%async_computation.5 | async-start | bytes 20971520 | tf_op jit(solution)/shard_map/all_gather | solution.py:171
  87.7 1.7 copy-start.5
  87.7 1.7 copy-start.10
  87.7 2.7 copy-start.3
  90.3 1.1 copy-start.6
  91.4 2.0 copy-start.2
  93.5 4.8 copy-start.7
  93.5 5.0 copy-start.9
  98.5 122.0 %copy-start.1 = (bf16[128,2048]{1,0:T(8,128)(2,1)}, bf16[128,2048]{1,0:T(8,128)(2,1)S(1)}, u32[]{:S(2)}) copy-start(bf16[128,2048]{1,0:T(8,128)(2,1)S(1)} %multiply_convert_fusion) | copy-start | bytes 1572868
  222.7 506.8 %all-reduce.3.cloned.1.call-start = ((), (), s32[]{:S(2)}) async-start(), calls=%async_computation.8 | async-start | bytes 33554432
  421.9 0.7 copy-start.14
  422.0 345.8 %all-gather.11.cloned.1.call-start = ((), (), s32[]{:S(2)}) async-start(), calls=%async_computation.6 | async-start | bytes 2621440 | tf_op jit(solution)/shard_map/all_gather | solution.py:172
  734.3 98.7 %all-to-all-start.1 = ((bf16[8,8,16,2048]{3,2,1,0:T(8,128)(2,1)}), bf16[8,8,16,2048]{3,2,1,0:T(8,128)(2,1)}, u32[]{:S(2)}, u32[]{:S(2)}) async-start(bf16[8,8,16,2048]{3,2,1,0:T(8,128)(2,1)} %copy.56), calls=%async_computation.1 | async-start | bytes 8388608 | tf_op jit(solution)/shard_map/all_to_all | solution.py:184
  738.9 117.1 %reduce-scatter.5.cloned.1.call-start = ((), (), s32[]{:S(2)}) async-start(), calls=%async_computation.7 | async-start | bytes 2621440 | tf_op jit(solution)/shard_map/reduce_scatter | solution.py:180
  770.7 5.7 copy-start.12
Sparse Core Ops, SparseCore 0:
  9.2 38.0 all-gather.4
  49.1 35.2 all-gather.6
  222.9 155.3 all-gather.8
  422.1 307.4 all-reduce.2
  731.4 36.3 all-gather.10
  776.5 35.1 reduce-scatter.4
where the time goes:
time: 872 us; the launch traced here: 865 us
  waiting for transfers between devices  607 us (70%)
  blocking collectives  98.9 us (11%)
  matrix products  64 us (7%)
  local copies, waits for them, and re-layouts  59.2 us (7%)
  other arithmetic  16.4 us (2%)
  between operations  14.8 us (2%)
    unnamed x7, waiting for transfers between devices  308 us
    all_gather x1, waiting for transfers between devices, on_device(): lax.all_gather(arrived, 'dp', axis=0, tiled=True)  155 us
    all_to_all x1, blocking collectives, on_device(): lax.all_to_all(outgoing, 'exp', split_axis=0, concat_axis=0, tiled=True)  98.9 us
    all_to_all x1, waiting for transfers between devices, on_device(): lax.all_to_all(routed_sum.astype(jnp.bfloat16), 'exp', split_axis=0, conc...  55.9 us
    all_gather x1, waiting for transfers between devices, on_device(): lax.all_gather(value_pool, 'dp', axis=0, tiled=True)  34 us
    all_gather x1, waiting for transfers between devices, on_device(): lax.all_gather(normed, 'dp', axis=0, tiled=True)  28.5 us
    dot_general x1, matrix products, expert_block(): jnp.einsum('sekf,efd->sekd', inner, down_rows, preferred_element_type=jnp...  26.4 us
    all_gather x1, waiting for transfers between devices, on_device(): lax.all_gather(key_pool, 'dp', axis=0, tiled=True)  25.3 us
  transfers between devices with their start and end apart: 7, of which 6 were waited for; matrix products, arithmetic and copies ran while one was open for 6% of the time, Pallas kernels for 0%

commit v1 on v0

--- a/solution.py
+++ b/solution.py
@@ -1,6 +1,8 @@
 import jax
 import jax.numpy as jnp
 from jax import lax
+from jax.experimental import pallas as pl
+from jax.experimental.pallas import tpu as pltpu
 from jax.sharding import PartitionSpec as P
 
 HEADS = 16
@@ -89,6 +91,397 @@
     upper_values = jnp.einsum("td,fd->tf", tokens, upper_rows, preferred_element_type=jnp.float32)
     inner = (jax.nn.silu(gate_values) * upper_values).astype(jnp.bfloat16)
     return jnp.dot(inner, down_rows, preferred_element_type=jnp.float32)
+
+
+MESH = pl.DeviceIdType.MESH
+Z_ORDER = (2, 3, 1, 0)
+
+
+def coordinates():
+    dp, col = lax.axis_index("dp"), lax.axis_index("exp")
+    row_x = dp + 1 - 2 * (dp % 2)
+    row_y = (dp + 2) % 4
+    row_d = (row_x + 2) % 4
+    core = col % 2
+    return dp, col, row_x, row_y, row_d, core
+
+
+def greet(dp, col, row_x, row_y, core):
+    barrier = pltpu.get_barrier_semaphore()
+    z = col // 2
+    partners = [(row_x, col), (row_y, col), (dp, z * 2 + 1 - core)]
+    partners += [(dp, ((z + dz) % 4) * 2 + core) for dz in (1, 2, 3)]
+    for partner in partners:
+        pl.semaphore_signal(barrier, inc=1, device_id=partner, device_id_type=MESH)
+    pl.semaphore_wait(barrier, 6)
+
+
+def spread_kernel(
+    own_ref, all_ref, local_sem, z_send, z_recv, x_send, x_recv, y_send, y_recv,
+    fx_send, fx_recv, fy_send, fy_recv, c_send, c_recv,
+):
+    dp, col, row_x, row_y, row_d, core = coordinates()
+    z = col // 2
+    sibling = z * 2 + 1 - core
+    half = own_ref.shape[0] // 2
+    greet(dp, col, row_x, row_y, core)
+
+    def remote(src, dst, send, recv, target):
+        return pltpu.make_async_remote_copy(
+            src_ref=src, dst_ref=dst, send_sem=send, recv_sem=recv,
+            device_id=target, device_id_type=MESH,
+        )
+
+    started = []
+
+    def go(copy):
+        copy.start()
+        started.append(copy)
+        return copy
+
+    local = pltpu.make_async_copy(own_ref, all_ref.at[dp, col], local_sem)
+    local.start()
+    z_copies = [None] * 4
+    x_copies, y_copies, fx_copies, fy_copies = [], [], [], []
+
+    def column(dz):
+        return ((z - dz + 4) % 4) * 2 + core
+
+    def first(dz):
+        if dz:
+            z_copies[dz].wait_recv()
+        where = column(dz)
+        src = all_ref.at[dp, where] if dz else own_ref
+        dst = all_ref.at[dp, where]
+        x_copies.append(go(remote(src, dst, x_send.at[dz], x_recv.at[dz], (row_x, col))))
+        y_copies.append(go(remote(src, dst, y_send.at[dz], y_recv.at[dz], (row_y, col))))
+        if dz == 0:
+            for step in (1, 2, 3):
+                target = (dp, ((z + step) % 4) * 2 + core)
+                z_copies[step] = go(
+                    remote(own_ref, dst, z_send.at[step], z_recv.at[step], target)
+                )
+        go(remote(src, dst, c_send.at[dz, 0], c_recv.at[dz, 0], (dp, sibling)))
+
+    def second(dz):
+        where = column(dz)
+        x_copies[dz].wait_recv()
+        block = all_ref.at[row_x, where]
+        part = all_ref.at[row_x, where, pl.ds(0, half)]
+        fy_copies.append(go(remote(part, part, fy_send.at[dz], fy_recv.at[dz], (row_y, col))))
+        go(remote(block, block, c_send.at[dz, 1], c_recv.at[dz, 1], (dp, sibling)))
+        y_copies[dz].wait_recv()
+        block = all_ref.at[row_y, where]
+        part = all_ref.at[row_y, where, pl.ds(half, half)]
+        fx_copies.append(go(remote(part, part, fx_send.at[dz], fx_recv.at[dz], (row_x, col))))
+        go(remote(block, block, c_send.at[dz, 2], c_recv.at[dz, 2], (dp, sibling)))
+
+    def third(dz):
+        fy_copies[dz].wait_recv()
+        fx_copies[dz].wait_recv()
+        block = all_ref.at[row_d, column(dz)]
+        go(remote(block, block, c_send.at[dz, 3], c_recv.at[dz, 3], (dp, sibling)))
+
+    for step in range(6):
+        if step < 4:
+            first(step)
+        if 1 <= step < 5:
+            second(step - 1)
+        if step >= 2:
+            third(step - 2)
+    local.wait()
+    for copy in started:
+        copy.wait_send()
+    rows = (dp, row_x, row_y, row_d)
+    for dz in range(4):
+        for k in range(4):
+            block = all_ref.at[rows[k], ((z - dz + 4) % 4) * 2 + 1 - core]
+            remote(block, block, c_send.at[dz, k], c_recv.at[dz, k], (dp, sibling)).wait_recv()
+
+
+def spread(normed):
+    rows, width = normed.shape
+    dma = pltpu.SemaphoreType.DMA
+    return pl.pallas_call(
+        spread_kernel,
+        out_shape=jax.ShapeDtypeStruct((4, 8, rows, width), normed.dtype),
+        in_specs=[pl.BlockSpec(memory_space=pl.ANY)],
+        out_specs=pl.BlockSpec(memory_space=pl.ANY),
+        scratch_shapes=[dma] + [dma((4,))] * 10 + [dma((4, 4))] * 2,
+        compiler_params=pltpu.CompilerParams(collective_id=1, has_side_effects=True),
+        name="spread_tokens",
+    )(normed)
+
+
+def collect_kernel(
+    part_ref, residual_ref, out_ref, acc, from_core, half_x, half_y, full_x, full_y, from_z,
+    load_sem, c_send, c_recv, hx_send, hx_recv, hy_send, hy_recv, x_send, x_recv, y_send, y_recv,
+    z_send, z_recv,
+):
+    dp, col, row_x, row_y, row_d, core = coordinates()
+    z = col // 2
+    sibling = z * 2 + 1 - core
+    rows = residual_ref.shape[0]
+    half = rows // 2
+    chunk = 16
+    greet(dp, col, row_x, row_y, core)
+    owners = (dp, row_x, row_y, row_d)
+
+    def remote(src, dst, send, recv, target):
+        return pltpu.make_async_remote_copy(
+            src_ref=src, dst_ref=dst, send_sem=send, recv_sem=recv,
+            device_id=target, device_id_type=MESH,
+        )
+
+    loads, crossings, started = {}, {}, []
+    halves_x, halves_y, fulls_x, fulls_y, z_copies = {}, {}, {}, {}, {}
+
+    def fetch(dz, k):
+        column = ((z + dz) % 4) * 2
+        crossing = remote(
+            part_ref.at[owners[k], column + 1 - core], from_core.at[dz, k],
+            c_send.at[dz, k], c_recv.at[dz, k], (dp, sibling),
+        )
+        crossing.start()
+        crossings[dz, k] = crossing
+        started.append(crossing)
+        load = pltpu.make_async_copy(
+            part_ref.at[owners[k], column + core], acc.at[dz, k], load_sem.at[dz, k]
+        )
+        load.start()
+        loads[dz, k] = load
+
+    def go(copy):
+        copy.start()
+        started.append(copy)
+        return copy
+
+    def wide(ref):
+        return ref[...].astype(jnp.float32)
+
+    def join(dz, k):
+        loads[dz, k].wait()
+        crossings[dz, k].wait_recv()
+
+    def add(dz, k, start, size, extras):
+        @pl.loop(0, size // chunk)
+        def _(i):
+            at = pl.ds(pl.multiple_of(start + i * chunk, chunk), chunk)
+            total = wide(acc.at[dz, k, at]) + wide(from_core.at[dz, k, at])
+            for extra, shift in extras:
+                total += wide(extra.at[pl.ds(pl.multiple_of(start - shift + i * chunk, chunk), chunk)])
+            acc[dz, k, at] = total.astype(acc.dtype)
+
+    for step in range(6):
+        if step < 4:
+            fetch(Z_ORDER[step], 3)
+        if 1 <= step < 5:
+            fetch(Z_ORDER[step - 1], 1)
+            fetch(Z_ORDER[step - 1], 2)
+        if step >= 2:
+            fetch(Z_ORDER[step - 2], 0)
+
+    def first(dz):
+        join(dz, 3)
+        add(dz, 3, 0, rows, [])
+        halves_x[dz] = go(remote(
+            acc.at[dz, 3, pl.ds(0, half)], half_x.at[dz], hx_send.at[dz], hx_recv.at[dz], (row_x, col)
+        ))
+        halves_y[dz] = go(remote(
+            acc.at[dz, 3, pl.ds(half, half)], half_y.at[dz], hy_send.at[dz], hy_recv.at[dz], (row_y, col)
+        ))
+
+    def second(dz):
+        join(dz, 1)
+        add(dz, 1, 0, half, [])
+        halves_y[dz].wait_recv()
+        add(dz, 1, half, half, [(half_y.at[dz], half)])
+        fulls_x[dz] = go(remote(acc.at[dz, 1], full_x.at[dz], x_send.at[dz], x_recv.at[dz], (row_x, col)))
+        join(dz, 2)
+        add(dz, 2, half, half, [])
+        halves_x[dz].wait_recv()
+        add(dz, 2, 0, half, [(half_x.at[dz], 0)])
+        fulls_y[dz] = go(remote(acc.at[dz, 2], full_y.at[dz], y_send.at[dz], y_recv.at[dz], (row_y, col)))
+
+    def third(dz):
+        join(dz, 0)
+        fulls_x[dz].wait_recv()
+        fulls_y[dz].wait_recv()
+        if dz:
+            add(dz, 0, 0, rows, [(full_x.at[dz], 0), (full_y.at[dz], 0)])
+            target = (dp, ((z + dz) % 4) * 2 + core)
+            z_copies[dz] = go(remote(
+                acc.at[dz, 0], from_z.at[dz - 1], z_send.at[dz - 1], z_recv.at[dz - 1], target
+            ))
+        else:
+            for copy in z_copies.values():
+                copy.wait_recv()
+
+            @pl.loop(0, rows // chunk)
+            def _(i):
+                at = pl.ds(pl.multiple_of(i * chunk, chunk), chunk)
+                total = wide(acc.at[0, 0, at]) + wide(from_core.at[0, 0, at])
+                total += wide(full_x.at[0, at]) + wide(full_y.at[0, at])
+                for k in range(3):
+                    total += wide(from_z.at[k, at])
+                out_ref[at] = (total + wide(residual_ref.at[at])).astype(out_ref.dtype)
+
+    for step in range(6):
+        if step < 4:
+            first(Z_ORDER[step])
+        if 1 <= step < 5:
+            second(Z_ORDER[step - 1])
+        if step >= 2:
+            third(Z_ORDER[step - 2])
+    for copy in started:
+        copy.wait_send()
+
+
+def collect(parts, residual):
+    rows, width = residual.shape
+    dtype = residual.dtype
+    dma = pltpu.SemaphoreType.DMA
+    vmem = pl.BlockSpec(memory_space=pltpu.VMEM)
+    return pl.pallas_call(
+        collect_kernel,
+        out_shape=jax.ShapeDtypeStruct((rows, width), dtype),
+        in_specs=[pl.BlockSpec(memory_space=pl.ANY), vmem],
+        out_specs=vmem,
+        scratch_shapes=[
+            pltpu.VMEM((4, 4, rows, width), dtype),
+            pltpu.VMEM((4, 4, rows, width), dtype),
+            pltpu.VMEM((4, rows // 2, width), dtype),
+            pltpu.VMEM((4, rows // 2, width), dtype),
+            pltpu.VMEM((4, rows, width), dtype),
+            pltpu.VMEM((4, rows, width), dtype),
+            pltpu.VMEM((3, rows, width), dtype),
+        ] + [dma((4, 4))] * 3 + [dma((4,))] * 8 + [dma((3,))] * 2,
+        compiler_params=pltpu.CompilerParams(
+            collective_id=2, has_side_effects=True, vmem_limit_bytes=48 * 2**20
+        ),
+        name="collect_sums",
+    )(parts, residual)
+
+
+def experts_kernel(
+    col_ref, tokens_ref, route_ref, gate_ref, up_ref, down_ref, sgate_ref, sup_ref, sdown_ref,
+    parts_ref, grouped, shared,
+):
+    step = pl.program_id(0)
+    col = col_ref[0]
+    local_experts, slots_all, width = grouped.shape
+    groups, tok_rows = tokens_ref.shape[0], tokens_ref.shape[2]
+    picks = route_ref.shape[2] // 2
+    slots = local_experts * CAP
+    columns = slots_all // CAP // groups
+    last = columns + local_experts
+
+    def match(group, weighted):
+        slot_ids = lax.broadcasted_iota(jnp.int32, (slots, tok_rows), 0)
+        slot_ids = (slot_ids + col * slots).astype(jnp.float32)
+        total = jnp.zeros((slots, tok_rows), jnp.float32)
+        for k in range(picks):
+            value = route_ref[group, 0, picks + k : picks + k + 1, :] if weighted else 1.0
+            total += jnp.where(slot_ids == route_ref[group, 0, k : k + 1, :], value, 0.0)
+        return total.astype(jnp.bfloat16)
+
+    def two_layers(rows, gate, up, down):
+        gates = lax.dot_general(
+            rows, gate, (((1,), (1,)), ((), ())), preferred_element_type=jnp.float32
+        )
+        ups = lax.dot_general(rows, up, (((1,), (1,)), ((), ())), preferred_element_type=jnp.float32)
+        inner = (gates / (1.0 + jnp.exp(-gates)) * ups).astype(jnp.bfloat16)
+        return jnp.dot(inner, down, preferred_element_type=jnp.float32).astype(jnp.bfloat16)
+
+    @pl.when(step < columns)
+    def _():
+        for group in range(groups):
+            at = pl.ds(pl.multiple_of((step * groups + group) * CAP, CAP), CAP)
+            rows = jnp.dot(
+                match(group, False), tokens_ref[group, 0], preferred_element_type=jnp.float32
+            ).astype(jnp.bfloat16)
+            for e in range(local_experts):
+                grouped[e, at, :] = rows[e * CAP : (e + 1) * CAP]
+
+        @pl.when(step == col)
+        def _():
+            for group in range(groups):
+                shared[group * tok_rows : (group + 1) * tok_rows, :] = tokens_ref[group, 0]
+
+    @pl.when((step >= columns) & (step < last))
+    def _():
+        expert = step - columns
+        grouped[expert] = two_layers(grouped[expert], gate_ref[0], up_ref[0], down_ref[0])
+
+    @pl.when(step == last)
+    def _():
+        shared[...] = two_layers(shared[...], sgate_ref[...], sup_ref[...], sdown_ref[...])
+
+    @pl.when(step > last)
+    def _():
+        column = step - last - 1
+        here = jnp.where(column == col, 1.0, 0.0)
+        for group in range(groups):
+            at = pl.ds(pl.multiple_of((column * groups + group) * CAP, CAP), CAP)
+            rows = jnp.concatenate([grouped[e, at, :] for e in range(local_experts)], axis=0)
+            sums = lax.dot_general(
+                match(group, True), rows, (((0,), (0,)), ((), ())), preferred_element_type=jnp.float32
+            )
+            own = shared[group * tok_rows : (group + 1) * tok_rows, :].astype(jnp.float32)
+            parts_ref[group, 0] = (sums + here * own).astype(jnp.bfloat16)
+
+
+def run_experts(tokens, routes, gate, up, down, sgate, sup, sdown):
+    groups, columns, tok_rows, width = tokens.shape
+    local_experts, units, _ = gate.shape
+    route_rows = routes.shape[2]
+    last = columns + local_experts
+    col = lax.axis_index("exp").astype(jnp.int32).reshape(1)
+
+    def column_in(i, col_ref):
+        j = jnp.where(i > last, i - last - 1, jnp.minimum(i, columns - 1))
+        return (0, j, 0, 0)
+
+    def tokens_in(i, col_ref):
+        return (0, jnp.minimum(i, columns - 1), 0, 0)
+
+    def expert_in(i, col_ref):
+        return (jnp.clip(i - columns, 0, local_experts - 1), 0, 0)
+
+    def parts_out(i, col_ref):
+        return (0, jnp.clip(i - last - 1, 0, columns - 1), 0, 0)
+
+    def shared_in(i, col_ref):
+        return (0, 0)
+
+    once = pl.Buffered(1)
+    return pl.pallas_call(
+        experts_kernel,
+        out_shape=jax.ShapeDtypeStruct(tokens.shape, tokens.dtype),
+        grid_spec=pltpu.PrefetchScalarGridSpec(
+            num_scalar_prefetch=1,
+            grid=(last + 1 + columns,),
+            in_specs=[
+                pl.BlockSpec((groups, 1, tok_rows, width), tokens_in),
+                pl.BlockSpec((groups, 1, route_rows, tok_rows), column_in),
+                pl.BlockSpec((1, units, width), expert_in),
+                pl.BlockSpec((1, units, width), expert_in),
+                pl.BlockSpec((1, units, width), expert_in),
+                pl.BlockSpec(sgate.shape, shared_in, pipeline_mode=once),
+                pl.BlockSpec(sup.shape, shared_in, pipeline_mode=once),
+                pl.BlockSpec(sdown.shape, shared_in, pipeline_mode=once),
+            ],
+            out_specs=pl.BlockSpec((groups, 1, tok_rows, width), parts_out),
+            scratch_shapes=[
+                pltpu.VMEM((local_experts, columns * groups * CAP, width), jnp.bfloat16),
+                pltpu.VMEM((groups * tok_rows, width), jnp.bfloat16),
+            ],
+        ),
+        compiler_params=pltpu.CompilerParams(
+            dimension_semantics=("arbitrary",), vmem_limit_bytes=60 * 2**20
+        ),
+        name="experts",
+    )(col, tokens, routes, gate, up, down, sgate, sup, sdown)
 
 
 def on_device(
@@ -112,6 +505,22 @@
     expert_weights,
 ):
     tok_rows, model_width = hidden.shape
+    local_experts = expert_gate.shape[0]
+    column_count = lax.axis_size("exp")
+    expert_count = local_experts * column_count
+    pick_count = expert_ids.shape[1]
+    flat_experts = expert_ids.reshape(-1)
+    onehot = (flat_experts[:, None] == jnp.arange(expert_count, dtype=jnp.int32)[None, :]).astype(
+        jnp.int32
+    )
+    slot_ids = jnp.sum((jnp.cumsum(onehot, axis=0) - 1) * onehot, axis=1)
+    destinations = flat_experts * CAP + slot_ids
+    small_slice = column_count == 8 and lax.axis_size("dp") == 4
+    if small_slice:
+        route = jnp.concatenate(
+            [destinations.reshape(tok_rows, pick_count).astype(jnp.float32), expert_weights], axis=1
+        ).T
+        routes = lax.all_gather(route, ("dp", "exp")).reshape(4, 8, 2 * pick_count, tok_rows)
     local_requests, draft_nodes = parents.shape
     group_size = HEADS // KVH
     query_heads = queries.reshape(local_requests, draft_nodes, KVH, group_size, HD)
@@ -149,16 +558,11 @@
         jnp.mean(residual_wide * residual_wide, axis=-1, keepdims=True) + NORM_EPSILON
     )
     normed = (residual_wide * scale_rows * norm_gain.astype(jnp.float32)).astype(jnp.bfloat16)
-    local_experts = expert_gate.shape[0]
-    column_count = lax.axis_size("exp")
-    expert_count = local_experts * column_count
-    pick_count = expert_ids.shape[1]
-    flat_experts = expert_ids.reshape(-1)
-    onehot = (flat_experts[:, None] == jnp.arange(expert_count, dtype=jnp.int32)[None, :]).astype(
-        jnp.int32
-    )
-    slot_ids = jnp.sum((jnp.cumsum(onehot, axis=0) - 1) * onehot, axis=1)
-    destinations = flat_experts * CAP + slot_ids
+    if small_slice:
+        parts = run_experts(
+            spread(normed), routes, expert_gate, expert_up, expert_down, shared_gate, shared_up, shared_down
+        )
+        return collect(parts, residual)
     token_rows = jnp.arange(tok_rows * pick_count, dtype=jnp.int32) // pick_count
     outgoing = (
         jnp.zeros((expert_count * CAP, model_width), jnp.bfloat16)

time: 872 us -> 332 us (0.38)
  waiting for transfers between devices: 607 us -> 18.9 us
  Pallas kernels: 0 us -> 225 us
  matrix products: 64 us -> 10.3 us
  blocking collectives: 98.9 us -> 47.5 us
  local copies, waits for them, and re-layouts: 59.2 us -> 8.78 us
  other arithmetic: 16.4 us -> 6.95 us
    unnamed x7 -> x2, waiting for transfers between devices: 308 us -> 1.41 us
    pallas_call x0 -> x3, Pallas kernels: none -> 225 us  [the longest x1 87.6 us: collect(): pl.pallas_call(collect_kernel, out_shape=jax.ShapeDtypeStruct((rows, widt...]
    all_gather x2 -> x0, waiting for transfers between devices: 184 us -> none  [the longest x1 155 us: on_device(): lax.all_gather(arrived, 'dp', axis=0, tiled=True)]
    all_to_all x1 -> x0, blocking collectives: 98.9 us -> none  [on_device(): lax.all_to_all(outgoing, 'exp', split_axis=0, concat_axis=0, tiled=True)]
    all_to_all x1 -> x0, waiting for transfers between devices: 55.9 us -> none  [on_device(): lax.all_to_all(routed_sum.astype(jnp.bfloat16), 'exp', split_axis=0, conc...]
    dot_general x4 -> x0, matrix products: 52.3 us -> none  [the longest x1 26.4 us: expert_block(): jnp.einsum('sekf,efd->sekd', inner, down_rows, preferred_element_type=jnp...]
    all_gather x0 -> x1, blocking collectives: none -> 47.5 us  [on_device(): lax.all_gather(route, ('dp', 'exp')).reshape(4, 8, 2 * pick_count, tok_rows)]
    all_gather x1, waiting for transfers between devices: 25.3 us -> 0.02 us  [on_device(): lax.all_gather(key_pool, 'dp', axis=0, tiled=True)]
  transfers between devices with their start and end apart: 7 -> 2, of which waited for: 6 -> 1; matrix products, arithmetic and copies ran while one was open for 6% -> 4% of each run, Pallas kernels for 0% -> 0%
where the time goes in v1:
time: 332 us; the launch traced here: 331 us
  Pallas kernels  225 us (68%)
  blocking collectives  47.5 us (14%)
  waiting for transfers between devices  18.9 us (6%)
  between operations  13.7 us (4%)
  matrix products  10.3 us (3%)
  local copies, waits for them, and re-layouts  8.78 us (3%)
  other arithmetic  6.95 us (2%)
    pallas_call x1, Pallas kernels, collect(): pl.pallas_call(collect_kernel, out_shape=jax.ShapeDtypeStruct((rows, widt...  87.6 us
    pallas_call x1, Pallas kernels, spread(): pl.pallas_call(spread_kernel, out_shape=jax.ShapeDtypeStruct((4, 8, rows,...  82.7 us
    pallas_call x1, Pallas kernels, run_experts(): pl.pallas_call(experts_kernel, out_shape=jax.ShapeDtypeStruct(tokens.shap...  55 us
    all_gather x1, blocking collectives, on_device(): lax.all_gather(route, ('dp', 'exp')).reshape(4, 8, 2 * pick_count, tok_rows)  47.5 us
    all_gather x1, waiting for transfers between devices, on_device(): lax.all_gather(value_pool, 'dp', axis=0, tiled=True)  17.5 us
  transfers between devices with their start and end apart: 2, of which 1 were waited for; matrix products, arithmetic and copies ran while one was open for 4% of the time, Pallas kernels for 0%

profile of v1, /device:TPU:0, one launch (start us, length us, event | category | flops | bytes accessed | tf_op | source)
XLA Modules:
  0.0 331.4 jit_solution(2034166247238132560)
XLA Ops:
  6.5 0.0 copy-start.2
  6.5 0.0 all-gather.5.cloned.1.call-start
  6.5 0.7 all-gather.5.cloned.1.call-update
  7.3 0.0 copy-start.1
  7.3 0.0 all-gather.7.cloned.1.call-start
  7.3 0.7 all-gather.7.cloned.1.call-update
  8.0 0.7 compare_and_fusion.1
  8.7 0.7 compare_select_fusion
  9.4 0.8 copy.65
  10.2 0.1 eq.53
  10.3 0.1 eq.49
  10.5 0.1 broadcast_in_dim.75
  10.5 0.1 reshape.75
  10.6 0.1 reshape.82
  10.7 1.3 convert_element_type.54
  12.0 1.0 convolution_minimum_fusion.5
  13.1 0.0 copy-start.4
  13.1 0.0 copy-start.5
  13.1 0.2 convolution_minimum_fusion.4
  13.3 0.2 convolution_minimum_fusion.3
  13.5 0.0 copy-start.6
  13.5 0.2 convolution_minimum_fusion.2
  13.7 0.2 convolution_minimum_fusion.1
  13.9 0.2 fusion.12
  14.1 0.1 copy.56
  14.2 1.8 reduce-window.6
  16.0 0.3 slice_reduce_fusion
  16.3 0.1 fusion.35
  16.5 0.1 reduce_sum.48
  16.6 0.1 copy.68
  16.7 0.0 copy-done.2
  16.8 0.0 copy-done.1
  16.8 0.4 reshape.74
  17.2 0.0 copy-done.4
  17.2 0.0 copy-done.5
  17.2 47.5 %all-gather.1 = f32[32,12,128]{2,1,0:T(8,128)} all-gather(f32[1,12,128]{2,1,0:T(8,128)S(1)} %maximum_bitcast_fusion), channel_id=2, replica_groups=mesh['dp'=4,'exp'=8] {'dp','exp'}, dimensions={0}, use_global_device_ids=true | all-gather | bytes 202752 | tf_op jit(solution)/shard_map/all_gather | solution.py:523
  64.7 0.0 copy-done.6
  64.7 0.1 compare_and_fusion
  64.8 0.7 fusion.58
  65.5 0.0 all-gather.5.cloned.1.call-done
  65.5 2.2 gather_fusion
  67.7 0.1 reshape.76
  67.8 17.5 %all-gather.7.cloned.1.call-done = bf16[32,64,512]{2,1,0:T(8,128)(2,1)} async-done(((bf16[8,64,512]{2,1,0:T(8,128)(2,1)}), bf16[32,64,512]{2,1,0:T(8,128)(2,1)}) %all-gather.7.cloned.1.call-update) | async-done | bytes 2097168 | tf_op jit(solution)/shard_map/all_gather | solution.py:544
  85.3 2.2 gather_fusion.1
  87.5 0.1 reshape.77
  87.6 0.6 bitcast_reduce_fusion
  88.2 0.9 fusion.3
  89.1 1.0 convolution_bitcast_fusion.1
  90.1 0.3 fusion.23
  90.4 1.2 fusion.11
  91.6 0.0 copy-start
  91.6 0.4 copy.64
  92.0 0.4 convert_element_type.51
  92.4 0.2 copy-done
  92.7 0.0 copy-start.3
  92.7 4.8 %fusion.13 = (f32[128]{0:T(128)S(1)}, bf16[128,2048]{1,0:T(8,128)(2,1)S(1)}) fusion(bf16[128,2048]{1,0:T(8,128)(2,1)S(1)} %convert_element_type.51, bf16[2048,2048]{1,0:T(8,128)(2,1)} %param.26, bf16[128,2048]{1,0:T(8,128)(2,1)S(1)} %copy-done), kind=kOutput, calls=%fused_computation.30 | convolution fusion | flops 1075314560 | bytes 9961984 | tf_op jit(solution)/shard_map/dot_general | solution.py:554
  97.5 0.0 copy-done.3
  97.5 1.0 fusion.15.own_ref
  98.5 82.7 %spread_tokens.1.tokens_ref = bf16[4,8,128,2048]{3,2,1,0:T(8,128)(2,1)} custom-call(bf16[128,2048]{1,0:T(8,128)(2,1)} %fusion.15.own_ref), custom_call_target="tpu_custom_call" | custom-call | tf_op jit(solution)/shard_map/spread_tokens/pallas_call | solution.py:205
  181.2 55.0 %experts.1.part_ref = bf16[4,8,128,2048]{3,2,1,0:T(8,128)(2,1)} custom-call(s32[1]{0:T(128)} %bitcast.col_ref, bf16[4,8,128,2048]{3,2,1,0:T(8,128)(2,1)} %spread_tokens.1.tokens_ref, f32[4,8,12,128]{3,2,1,0:T(8,128)} %bitcast.89, bf16[8,352,2048]{2,1,0:T(8,128)(2,1)} %gate_ref.1, bf16[8,352,2048]{2,1,0:T(8,128)(2,1)} %up_ref.1, ...), custom_call_target="tpu_custom_call" | custom-call | tf_op jit(solution)/shard_map/experts/pallas_call | solution.py:458
  236.1 87.6 %collect_sums.1 = bf16[128,2048]{1,0:T(8,128)(2,1)S(1)} custom-call(bf16[4,8,128,2048]{3,2,1,0:T(8,128)(2,1)} %experts.1.part_ref, bf16[128,2048]{1,0:T(8,128)(2,1)S(1)} %get-tuple-element.17.residual_ref), custom_call_target="tpu_custom_call" | custom-call | tf_op jit(solution)/shard_map/collect_sums/pallas_call | solution.py:345
  323.7 0.8 copy.105
  (12 shorter events, 0.2 us)
Async XLA Ops:
  6.5 10.2 %copy-start.2 = (bf16[2,128,512]{2,1,0:T(8,128)(2,1)S(1)}, bf16[2,128,512]{2,1,0:T(8,128)(2,1)}, u32[]{:S(2)}) copy-start(bf16[2,128,512]{2,1,0:T(8,128)(2,1)} %param.20) | copy-start | bytes 786436
  6.5 58.9 %all-gather.5.cloned.1.call-start = ((), (), s32[]{:S(2)}) async-start(), calls=%async_computation | async-start | bytes 2621440 | tf_op jit(solution)/shard_map/all_gather | solution.py:543
  7.3 9.5 %copy-start.1 = (bf16[128,2048]{1,0:T(8,128)(2,1)S(1)}, bf16[128,2048]{1,0:T(8,128)(2,1)}, u32[]{:S(2)}) copy-start(bf16[128,2048]{1,0:T(8,128)(2,1)} %param.19) | copy-start | bytes 1572868
  7.3 78.0 %all-gather.7.cloned.1.call-start = ((), (), s32[]{:S(2)}) async-start(), calls=%async_computation.1 | async-start | bytes 2621440 | tf_op jit(solution)/shard_map/all_gather | solution.py:544
  13.1 4.1 %copy-start.4 = (s32[128,6]{0,1:T(8,128)S(1)}, s32[128,6]{0,1:T(8,128)}, u32[]{:S(2)}) copy-start(s32[128,6]{0,1:T(8,128)} %param.34) | copy-start | bytes 9220
  13.1 4.1 %copy-start.5 = (f32[128,6]{0,1:T(8,128)S(1)}, f32[128,6]{0,1:T(8,128)}, u32[]{:S(2)}) copy-start(f32[128,6]{0,1:T(8,128)} %param.35) | copy-start | bytes 9220
  13.5 51.2 %copy-start.6 = (s32[2]{0:T(128)S(1)}, s32[2]{0:T(128)}, u32[]{:S(2)}) copy-start(s32[2]{0:T(128)} %param.24) | copy-start | bytes 28
  91.6 1.0 copy-start
  92.7 4.8 %copy-start.3 = (f32[2048]{0:T(1024)S(1)}, f32[2048]{0:T(1024)}, u32[]{:S(2)}) copy-start(f32[2048]{0:T(1024)} %convert_element_type.54) | copy-start | bytes 24580
Sparse Core Ops, SparseCore 0:
  9.2 38.8 all-gather.4
  49.9 35.3 all-gather.6

commit v2 on v1

--- a/solution.py
+++ b/solution.py
@@ -116,7 +116,68 @@
     pl.semaphore_wait(barrier, 6)
 
 
-def spread_kernel(
+def spread_kernel(own_ref, all_ref, *sems):
+    dp, col, row_x, row_y, row_d, core = coordinates()
+    greet(dp, col, row_x, row_y, core)
+    spread_block(own_ref, all_ref, *sems)
+
+
+def pages_kernel(
+    route_ref, key_ref, value_ref, routes_ref, keys_ref, values_ref, load_sem, x_send, x_recv,
+    y_send, y_recv, fx_send, fx_recv, fy_send, fy_recv, *sems,
+):
+    dp, col, row_x, row_y, row_d, core = coordinates()
+    half = key_ref.shape[0] // 2
+    greet(dp, col, row_x, row_y, core)
+
+    def send(src, dst, send_sem, recv_sem, row):
+        copy = pltpu.make_async_remote_copy(
+            src_ref=src, dst_ref=dst, send_sem=send_sem, recv_sem=recv_sem,
+            device_id=(row, col), device_id_type=MESH,
+        )
+        copy.start()
+        return copy
+
+    pools = ((key_ref, keys_ref), (value_ref, values_ref))
+    to_x, to_y, on_x, on_y, local = [], [], [], [], []
+    for i, (own, pool) in enumerate(pools):
+        to_x.append(send(own, pool.at[dp], x_send.at[i], x_recv.at[i], row_x))
+        to_y.append(send(own, pool.at[dp], y_send.at[i], y_recv.at[i], row_y))
+    for i, (own, pool) in enumerate(pools):
+        local.append(pltpu.make_async_copy(own, pool.at[dp], load_sem.at[i]))
+        local[i].start()
+    for i, (own, pool) in enumerate(pools):
+        to_x[i].wait_recv()
+        part = pool.at[row_x, pl.ds(0, half)]
+        on_y.append(send(part, part, fy_send.at[i], fy_recv.at[i], row_y))
+        to_y[i].wait_recv()
+        part = pool.at[row_y, pl.ds(half, half)]
+        on_x.append(send(part, part, fx_send.at[i], fx_recv.at[i], row_x))
+    spread_block(route_ref, routes_ref, *sems)
+    for i in range(2):
+        local[i].wait()
+        to_x[i].wait_send()
+        to_y[i].wait_send()
+        on_x[i].wait()
+        on_y[i].wait()
+
+
+def share_pages(route, keys, values):
+    dma = pltpu.SemaphoreType.DMA
+    anywhere = pl.BlockSpec(memory_space=pl.ANY)
+    pool = jax.ShapeDtypeStruct((4,) + keys.shape, keys.dtype)
+    return pl.pallas_call(
+        pages_kernel,
+        out_shape=[jax.ShapeDtypeStruct((4, 8) + route.shape, route.dtype), pool, pool],
+        in_specs=[anywhere] * 3,
+        out_specs=[anywhere] * 3,
+        scratch_shapes=[dma((2,))] * 9 + [dma] + [dma((4,))] * 10 + [dma((4, 4))] * 2,
+        compiler_params=pltpu.CompilerParams(collective_id=3, has_side_effects=True),
+        name="share_pages",
+    )(route, keys, values)
+
+
+def spread_block(
     own_ref, all_ref, local_sem, z_send, z_recv, x_send, x_recv, y_send, y_recv,
     fx_send, fx_recv, fy_send, fy_recv, c_send, c_recv,
 ):
@@ -124,7 +185,6 @@
     z = col // 2
     sibling = z * 2 + 1 - core
     half = own_ref.shape[0] // 2
-    greet(dp, col, row_x, row_y, core)
 
     def remote(src, dst, send, recv, target):
         return pltpu.make_async_remote_copy(
@@ -365,7 +425,7 @@
 
 def experts_kernel(
     col_ref, tokens_ref, route_ref, gate_ref, up_ref, down_ref, sgate_ref, sup_ref, sdown_ref,
-    parts_ref, grouped, shared,
+    parts_ref, grouped, shared, joined,
 ):
     step = pl.program_id(0)
     col = col_ref[0]
@@ -386,10 +446,14 @@
         return total.astype(jnp.bfloat16)
 
     def two_layers(rows, gate, up, down):
-        gates = lax.dot_general(
-            rows, gate, (((1,), (1,)), ((), ())), preferred_element_type=jnp.float32
-        )
-        ups = lax.dot_general(rows, up, (((1,), (1,)), ((), ())), preferred_element_type=jnp.float32)
+        units = gate.shape[0]
+        offset = joined.shape[0] - units
+        joined[0:units, :] = gate
+        joined[offset : offset + units, :] = up
+        both = lax.dot_general(
+            rows, joined[...], (((1,), (1,)), ((), ())), preferred_element_type=jnp.float32
+        )
+        gates, ups = both[:, 0:units], both[:, offset : offset + units]
         inner = (gates / (1.0 + jnp.exp(-gates)) * ups).astype(jnp.bfloat16)
         return jnp.dot(inner, down, preferred_element_type=jnp.float32).astype(jnp.bfloat16)
 
@@ -475,6 +539,7 @@
             scratch_shapes=[
                 pltpu.VMEM((local_experts, columns * groups * CAP, width), jnp.bfloat16),
                 pltpu.VMEM((groups * tok_rows, width), jnp.bfloat16),
+                pltpu.VMEM((-(-units // 128) * 128 + units, width), jnp.bfloat16),
             ],
         ),
         compiler_params=pltpu.CompilerParams(
@@ -517,10 +582,21 @@
     destinations = flat_experts * CAP + slot_ids
     small_slice = column_count == 8 and lax.axis_size("dp") == 4
     if small_slice:
+        spare = -pick_count % 8
+        places = destinations.reshape(tok_rows, pick_count).astype(jnp.float32).T
         route = jnp.concatenate(
-            [destinations.reshape(tok_rows, pick_count).astype(jnp.float32), expert_weights], axis=1
-        ).T
-        routes = lax.all_gather(route, ("dp", "exp")).reshape(4, 8, 2 * pick_count, tok_rows)
+            [
+                jnp.pad(places, ((0, spare), (0, 0)), constant_values=-1.0),
+                jnp.pad(expert_weights.T, ((0, spare), (0, 0))),
+            ],
+            axis=0,
+        )
+        routes, all_keys, all_values = share_pages(route, key_pool, value_pool)
+        all_keys = all_keys.reshape((-1,) + key_pool.shape[1:])
+        all_values = all_values.reshape((-1,) + value_pool.shape[1:])
+    else:
+        all_keys = lax.all_gather(key_pool, "dp", axis=0, tiled=True)
+        all_values = lax.all_gather(value_pool, "dp", axis=0, tiled=True)
     local_requests, draft_nodes = parents.shape
     group_size = HEADS // KVH
     query_heads = queries.reshape(local_requests, draft_nodes, KVH, group_size, HD)
@@ -539,10 +615,7 @@
         query_heads,
         page_table,
         cache_len,
-        (
-            lax.all_gather(key_pool, "dp", axis=0, tiled=True),
-            lax.all_gather(value_pool, "dp", axis=0, tiled=True),
-        ),
+        (all_keys, all_values),
     )
     attention = (
         (final_sum / jnp.transpose(final_total, (0, 3, 1, 2))[..., None])

time: 332 us -> 309 us (0.931)
  Pallas kernels: 225 us -> 282 us
  blocking collectives: 47.5 us -> 0 us
  waiting for transfers between devices: 18.9 us -> 0 us
  between operations: 13.7 us -> 0.26 us
    pallas_call x0 -> x1, Pallas kernels: none -> 52.7 us  [share_pages(): pl.pallas_call(pages_kernel, out_shape=[jax.ShapeDtypeStruct((4, 8) + rou...]
    all_gather x1 -> x0, blocking collectives: 47.5 us -> none  [on_device(): lax.all_gather(route, ('dp', 'exp')).reshape(4, 8, 2 * pick_count, tok_rows)]
    all_gather x2 -> x0, waiting for transfers between devices: 17.5 us -> none  [the longest x1 17.5 us: on_device(): lax.all_gather(value_pool, 'dp', axis=0, tiled=True)]
    pallas_call x1, Pallas kernels: 55 us -> 60.7 us  [run_experts(): pl.pallas_call(experts_kernel, out_shape=jax.ShapeDtypeStruct(tokens.shap...]
  transfers between devices with their start and end apart: 2 -> 0, of which waited for: 1 -> 0; matrix products, arithmetic and copies ran while one was open for 4% -> 0% of each run, Pallas kernels for 0% -> 0%
where the time goes in v2:
time: 309 us
  Pallas kernels  282 us (91%)
  matrix products  10.1 us (3%)
  local copies, waits for them, and re-layouts  8.76 us (3%)
  other arithmetic  7.68 us (2%)
    pallas_call x1, Pallas kernels, collect(): pl.pallas_call(collect_kernel, out_shape=jax.ShapeDtypeStruct((rows, widt...  87.5 us
    pallas_call x1, Pallas kernels, spread(): pl.pallas_call(spread_kernel, out_shape=jax.ShapeDtypeStruct((4, 8, rows,...  81.1 us
    pallas_call x1, Pallas kernels, run_experts(): pl.pallas_call(experts_kernel, out_shape=jax.ShapeDtypeStruct(tokens.shap...  60.7 us
    pallas_call x1, Pallas kernels, share_pages(): pl.pallas_call(pages_kernel, out_shape=[jax.ShapeDtypeStruct((4, 8) + rou...  52.7 us

profile of v2, /device:TPU:0, one launch (start us, length us, event | category | flops | bytes accessed | tf_op | source)
XLA Modules:
  0.0 308.8 jit_solution(10468515542035996341)
XLA Ops:
  0.0 0.0 copy-start.3
  0.0 0.0 copy-start.4
  0.0 0.0 copy-start.2
  0.0 0.0 copy-start.1
  0.0 0.8 compare_and_fusion.1
  0.8 0.1 broadcast_in_dim.75
  0.8 0.1 reshape.78
  0.9 0.7 compare_and_fusion
  1.7 0.7 compare_select_fusion
  2.3 0.1 reshape.86
  2.4 0.7 convert_element_type.58
  3.1 1.0 convolution_minimum_fusion.5
  4.2 0.2 convolution_minimum_fusion.4
  4.4 0.2 convolution_minimum_fusion.3
  4.6 0.2 convolution_minimum_fusion.2
  4.8 0.2 convolution_minimum_fusion.1
  5.0 0.2 fusion.12
  5.2 0.1 copy.23
  5.3 0.8 copy.28
  6.1 0.1 eq.53
  6.2 0.1 eq.49
  6.4 1.8 reduce-window.6
  8.2 0.3 slice_reduce_fusion
  8.5 0.1 fusion.35
  8.6 0.1 reduce_sum.43
  8.8 0.1 copy.31
  8.8 0.0 copy-done.3
  8.8 0.0 copy-done.4
  8.9 0.6 select_maximum_fusion.route_ref
  9.5 0.0 copy-done.2
  9.6 0.0 copy-done.1
  9.6 0.4 reshape.77
  9.9 0.7 fusion.58
  10.6 52.7 %share_pages.1 = (f32[4,8,16,128]{3,2,1,0:T(8,128)}, bf16[4,8,64,512]{3,2,1,0:T(8,128)(2,1)}, bf16[4,8,64,512]{3,2,1,0:T(8,128)(2,1)}) custom-call(f32[16,128]{1,0:T(8,128)} %select_maximum_fusion.route_ref, bf16[8,64,512]{2,1,0:T(8,128)(2,1)} %key_ref.1, bf16[8,64,512]{2,1,0:T(8,128)(2,1)} %value_ref.1), custom_call_target="tpu_custom_call" | custom-call | tf_op jit(solution)/shard_map/share_pages/pallas_call | solution.py:169
  63.3 2.2 gather_fusion
  65.5 0.1 reshape.81
  65.6 2.2 gather_fusion.1
  67.8 0.1 reshape.83
  67.9 0.6 bitcast_reduce_fusion
  68.5 0.3 fusion.23
  68.8 0.9 fusion.3
  69.7 0.8 convolution_bitcast_fusion.1
  70.5 1.2 fusion.11
  71.8 0.0 copy-start
  71.8 0.4 copy.35
  72.2 0.4 convert_element_type.55
  72.6 0.2 copy-done
  72.8 4.8 %fusion.13 = (f32[128]{0:T(128)S(1)}, bf16[128,2048]{1,0:T(8,128)(2,1)S(1)}) fusion(bf16[128,2048]{1,0:T(8,128)(2,1)S(1)} %convert_element_type.55, bf16[2048,2048]{1,0:T(8,128)(2,1)} %param.26, bf16[128,2048]{1,0:T(8,128)(2,1)S(1)} %copy-done), kind=kOutput, calls=%fused_computation.30 | convolution fusion | flops 1075314560 | bytes 9961984 | tf_op jit(solution)/shard_map/dot_general | solution.py:627
  77.6 1.0 fusion.15.own_ref
  78.6 81.1 %spread_tokens.1.tokens_ref = bf16[4,8,128,2048]{3,2,1,0:T(8,128)(2,1)} custom-call(bf16[128,2048]{1,0:T(8,128)(2,1)} %fusion.15.own_ref), custom_call_target="tpu_custom_call" | custom-call | tf_op jit(solution)/shard_map/spread_tokens/pallas_call | solution.py:265
  159.8 60.7 %experts.1.part_ref = bf16[4,8,128,2048]{3,2,1,0:T(8,128)(2,1)} custom-call(s32[1]{0:T(128)} %bitcast.col_ref, bf16[4,8,128,2048]{3,2,1,0:T(8,128)(2,1)} %spread_tokens.1.tokens_ref, f32[4,8,16,128]{3,2,1,0:T(8,128)} %get-tuple-element.10.route_ref, bf16[8,352,2048]{2,1,0:T(8,128)(2,1)} %gate_ref.1, bf16[8,352,2048]{2,1,0:T(8,128)(2,1)} %up_ref.1, ...), custom_call_target="tpu_custom_call" | custom-call | tf_op jit(solution)/shard_map/experts/pallas_call | solution.py:522
  220.5 87.5 %collect_sums.1 = bf16[128,2048]{1,0:T(8,128)(2,1)S(1)} custom-call(bf16[4,8,128,2048]{3,2,1,0:T(8,128)(2,1)} %experts.1.part_ref, bf16[128,2048]{1,0:T(8,128)(2,1)S(1)} %get-tuple-element.23.residual_ref), custom_call_target="tpu_custom_call" | custom-call | tf_op jit(solution)/shard_map/collect_sums/pallas_call | solution.py:405
  308.0 0.8 copy.72
  (11 shorter events, 0.2 us)
Async XLA Ops:
  0.0 8.8 %copy-start.3 = (s32[128,6]{0,1:T(8,128)S(1)}, s32[128,6]{0,1:T(8,128)}, u32[]{:S(2)}) copy-start(s32[128,6]{0,1:T(8,128)} %param.34) | copy-start | bytes 9220
  0.0 8.9 %copy-start.4 = (f32[128,6]{0,1:T(8,128)S(1)}, f32[128,6]{0,1:T(8,128)}, u32[]{:S(2)}) copy-start(f32[128,6]{0,1:T(8,128)} %param.35) | copy-start | bytes 9220
  0.0 9.5 %copy-start.2 = (bf16[2,128,512]{2,1,0:T(8,128)(2,1)S(1)}, bf16[2,128,512]{2,1,0:T(8,128)(2,1)}, u32[]{:S(2)}) copy-start(bf16[2,128,512]{2,1,0:T(8,128)(2,1)} %param.20) | copy-start | bytes 786436
  0.0 9.6 %copy-start.1 = (bf16[128,2048]{1,0:T(8,128)(2,1)S(1)}, bf16[128,2048]{1,0:T(8,128)(2,1)}, u32[]{:S(2)}) copy-start(bf16[128,2048]{1,0:T(8,128)(2,1)} %param.19) | copy-start | bytes 1572868
  71.8 1.0 copy-start
